TPU v7x, 256 devices: a whole 4x4x8 slice. The times are simulated.
256 devices in a mesh: ab: 16 (over y, x_lo, core), cd: 16 (over z, x_hi).
Axes of the slice: x: 4 (x_hi: 2, x_lo: 2; x = x_hi * 2 + x_lo), y: 4, z: 8, core: 2. Of those that a mesh axis runs over, the one named last changes fastest.
Arguments:
- amplitudes: bfloat16 [128, 32768], P('ab', 'cd'), may hold values from -6 to 6
- integrals: bfloat16 [32768, 32768], P('ab', 'cd'), as said below
- vir_energy: float32 [32768], replicated, may hold values from 0.6 to 1.6
- occ_energy: float32 [128], replicated, may hold values from -0.5 to -0.1
Outputs:
- ladder_one: bfloat16 [128, 32768], P('cd', 'ab')
- ladder_two: bfloat16 [128, 32768], P('ab', 'cd')
- ladder_three: bfloat16 [128, 32768], P('cd', 'ab')
Inputs may be any that keep to these rules, and one draw needn't show every extreme that they name: integrals is symmetric: integrals[x, y] equals integrals[y, x].
All inputs are finite; a program needn't handle non-finite values.
Results may differ from a plain program's by a relative error of at most 0.02.
Values may be sent and summed in bfloat16 or wider, within the bound.
A program may use at most 64 MiB of HBM per device.

v0:
```python
import jax
import jax.numpy as jnp
from jax import lax
from jax.sharding import PartitionSpec as P


def gather_ab(amps):
    return lax.all_gather(amps, "ab", axis=0, tiled=True)


def scatter_cd(gathered, integrals):
    return lax.psum_scatter(
        lax.dot_general(
            gathered, integrals, (((1,), (1,)), ((), ())), preferred_element_type=jnp.float32
        ),
        "cd",
        scatter_dimension=0,
        tiled=True,
    )


def per_device(amplitudes, integrals, vir_energy, occ_energy):
    n_ab = lax.axis_size("ab")
    n_cd = lax.axis_size("cd")
    index_ab = lax.axis_index("ab")
    index_cd = lax.axis_index("cd")
    rows_total = amplitudes.shape[0] * n_ab
    rows_ab = rows_total // n_ab
    rows_cd = rows_total // n_cd
    width_ab = integrals.shape[0]
    width_cd = integrals.shape[1]
    vir_ab = lax.dynamic_slice_in_dim(vir_energy, index_ab * width_ab, width_ab, 0)
    vir_cd = lax.dynamic_slice_in_dim(vir_energy, index_cd * width_cd, width_cd, 0)
    occ_ab = lax.dynamic_slice_in_dim(occ_energy, index_ab * rows_ab, rows_ab, 0)
    occ_cd = lax.dynamic_slice_in_dim(occ_energy, index_cd * rows_cd, rows_cd, 0)
    denom_second = vir_ab[None, :] - occ_cd[:, None]
    denom_first = vir_cd[None, :] - occ_ab[:, None]
    sum_one = scatter_cd(gather_ab(amplitudes), integrals)
    step_one = (sum_one / denom_second).astype(jnp.bfloat16)
    gathered = lax.all_gather(step_one, "cd", axis=0, tiled=True)
    sum_two = lax.psum_scatter(
        jnp.dot(gathered, integrals, preferred_element_type=jnp.float32).astype(jnp.bfloat16),
        "ab",
        scatter_dimension=0,
        tiled=True,
    ).astype(jnp.float32)
    step_two = (sum_two / denom_first).astype(jnp.bfloat16)
    sum_three = scatter_cd(gather_ab(step_two), integrals)
    return (
        sum_one.astype(jnp.bfloat16),
        sum_two.astype(jnp.bfloat16),
        sum_three.astype(jnp.bfloat16),
    )


def solution(mesh):
    return jax.shard_map(
        per_device,
        mesh=mesh,
        in_specs=(P("ab", "cd"), P("ab", "cd"), P(), P()),
        out_specs=(P("cd", "ab"), P("ab", "cd"), P("cd", "ab")),
        check_vma=False,
    )
```

profile of v0, /device:TPU:8, one launch (start us, length us, event | category | flops | bytes accessed | tf_op | source)
XLA Modules:
  0.0 585.3 jit_solution(5083432838263310757)
XLA Ops:
  7.2 0.0 copy-start
  7.2 0.0 reduce-scatter.4.cloned.1.call-start
  7.2 19.6 %all_gather.9 = bf16[128,2048]{1,0:T(8,128)(2,1)S(1)} all-gather(bf16[8,2048]{1,0:T(8,128)(2,1)} %param.4), channel_id=1, replica_groups=mesh['ab'=16,'cd'=16] {'ab'}, dimensions={0}, use_global_device_ids=true | all-gather | bytes 557056 | tf_op jit(solution)/shard_map/all_gather | solution.py:8
  26.9 7.3 %fusion.2 = f32[128,2048]{1,0:T(8,128)} fusion(bf16[128,2048]{1,0:T(8,128)(2,1)S(1)} %all_gather.9, bf16[2048,2048]{1,0:T(8,128)(2,1)} %param.5), kind=kOutput, calls=%fused_computation.5 | convolution fusion | flops 1073741824 | bytes 9961472 | tf_op jit(solution)/shard_map/dot_general | solution.py:13
  34.1 0.0 reduce-scatter.4.cloned.1.call-update
  34.1 0.0 reduce-scatter.6.cloned.1.call-start
  34.2 0.0 copy-done
  34.2 0.1 fusion.1
  34.3 0.7 fusion
  35.0 204.7 %reduce-scatter.4.cloned.1.call-done = f32[8,2048]{1,0:T(8,128)} async-done(((f32[128,2048]{1,0:T(8,128)}), f32[8,2048]{1,0:T(8,128)}) %reduce-scatter.4.cloned.1.call-update) | async-done | bytes 65552 | tf_op jit(solution)/shard_map/reduce_scatter | solution.py:12
  239.7 1.5 divide_convert_fusion.1
  241.3 41.1 %all_gather.10 = bf16[128,2048]{1,0:T(8,128)(2,1)S(1)} all-gather(bf16[8,2048]{1,0:T(8,128)(2,1)S(1)} %get-tuple-element.5), channel_id=1, replica_groups=mesh['ab'=16,'cd'=16] {'cd'}, dimensions={0}, use_global_device_ids=true | all-gather | bytes 557056 | tf_op jit(solution)/shard_map/all_gather | solution.py:40
  282.4 5.5 convolution_convert_fusion
  287.9 0.0 reduce-scatter.6.cloned.1.call-update
  287.9 0.0 reduce-scatter.8.cloned.1.call-start
  287.9 54.0 %reduce-scatter.6.cloned.1.call-done = bf16[8,2048]{1,0:T(8,128)(2,1)} async-done(((bf16[128,2048]{1,0:T(8,128)(2,1)}), bf16[8,2048]{1,0:T(8,128)(2,1)}) %reduce-scatter.6.cloned.1.call-update) | async-done | bytes 32784 | tf_op jit(solution)/shard_map/reduce_scatter | solution.py:41
  341.9 0.8 divide_convert_fusion
  342.8 23.3 %all_gather.11 = bf16[128,2048]{1,0:T(8,128)(2,1)S(1)} all-gather(bf16[8,2048]{1,0:T(8,128)(2,1)S(1)} %divide_convert_fusion), channel_id=1, replica_groups=mesh['ab'=16,'cd'=16] {'ab'}, dimensions={0}, use_global_device_ids=true | all-gather | bytes 557056 | tf_op jit(solution)/shard_map/all_gather | solution.py:8
  366.0 7.3 %fusion.3 = f32[128,2048]{1,0:T(8,128)} fusion(bf16[128,2048]{1,0:T(8,128)(2,1)S(1)} %all_gather.11, bf16[2048,2048]{1,0:T(8,128)(2,1)} %param.5), kind=kOutput, calls=%fused_computation.6 | convolution fusion | flops 1073741824 | bytes 9961472 | tf_op jit(solution)/shard_map/dot_general | solution.py:13
  373.3 0.0 reduce-scatter.8.cloned.1.call-update
  373.3 204.0 %reduce-scatter.8.cloned.1.call-done = f32[8,2048]{1,0:T(8,128)} async-done(((f32[128,2048]{1,0:T(8,128)}), f32[8,2048]{1,0:T(8,128)}) %reduce-scatter.8.cloned.1.call-update) | async-done | bytes 65552 | tf_op jit(solution)/shard_map/reduce_scatter | solution.py:12
  577.3 1.5 convert_element_type.24
Async XLA Ops:
  7.2 27.0 %copy-start = (f32[128]{0:T(128)S(1)}, f32[128]{0:T(128)}, u32[]{:S(2)}) copy-start(f32[128]{0:T(128)} %param.7) | copy-start | bytes 1540
  7.2 232.6 %reduce-scatter.4.cloned.1.call-start = ((), (), s32[]{:S(2)}) async-start(), calls=%async_computation.3 | async-start | bytes 1114112 | tf_op jit(solution)/shard_map/reduce_scatter | solution.py:12
  34.1 307.8 %reduce-scatter.6.cloned.1.call-start = ((), (), s32[]{:S(2)}) async-start(), calls=%async_computation.4 | async-start | bytes 557056 | tf_op jit(solution)/shard_map/reduce_scatter | solution.py:41
  287.9 289.4 %reduce-scatter.8.cloned.1.call-start = ((), (), s32[]{:S(2)}) async-start(), calls=%async_computation.5 | async-start | bytes 1114112 | tf_op jit(solution)/shard_map/reduce_scatter | solution.py:12
Sparse Core Ops, SparseCore 0:
  34.3 205.4 reduce-scatter.3
  288.0 53.8 reduce-scatter.5
  373.4 203.8 reduce-scatter.7
where the time goes:
time: 586 us; the launch traced here: 585 us
  waiting for transfers between devices  463 us (79%)
  blocking collectives  84 us (14%)
  matrix products  20 us (3%)
  between operations  13.8 us (2%)
    reduce_scatter x2, waiting for transfers between devices, scatter_cd(): lax.psum_scatter(lax.dot_general(gathered, integrals, (((1,), (1,)), ((),...  409 us
    reduce_scatter x1, waiting for transfers between devices, per_device(): lax.psum_scatter(jnp.dot(gathered, integrals, preferred_element_type=jnp....  54 us
    all_gather x2, blocking collectives, gather_ab(): return lax.all_gather(amps, 'ab', axis=0, tiled=True)  42.9 us
    all_gather x1, blocking collectives, per_device(): gathered = lax.all_gather(step_one, 'cd', axis=0, tiled=True)  41.1 us
    dot_general x2, matrix products, scatter_cd(): lax.dot_general(gathered, integrals, (((1,), (1,)), ((), ())), preferred_...  14.5 us
  transfers between devices with their start and end apart: 3, of which 3 were waited for; matrix products, arithmetic and copies ran while one was open for 0% of the time, Pallas kernels for 0%

commit v1 on v0

v1 whole, which is shorter than its diff:
```python
import functools

import jax
import jax.numpy as jnp
from jax import lax
from jax.experimental import pallas as pl
from jax.experimental.pallas import tpu as pltpu
from jax.sharding import PartitionSpec as P

MESH = pl.DeviceIdType.MESH
F32 = jnp.float32
BF16 = jnp.bfloat16

GROUP = 8
LANES = 128
ROWS = 8
CHUNKS = 4
STAGES = (0, 4, 6, 9, 11)


class Axis:
    def __init__(self, name, other):
        self.name = name
        self.index = lax.axis_index(name)
        self.other = lax.axis_index(other)
        self.group = self.index // 2
        self.pair = self.index % 2

    def device(self, index):
        return (index, self.other) if self.name == "ab" else (self.other, index)

    def peer_group(self, k):
        return (self.group + k) % GROUP

    def source_group(self, k):
        return (self.group + GROUP - k) % GROUP

    def peer(self, k):
        return self.device(self.peer_group(k) * 2 + self.pair)

    def partner(self):
        return self.device(self.group * 2 + 1 - self.pair)


def remote(src, dst, send, recv, device):
    return pltpu.make_async_remote_copy(
        src_ref=src, dst_ref=dst, send_sem=send, recv_sem=recv, device_id=device, device_id_type=MESH
    )


def each_peer(body):
    def step(k, carry):
        body(k)
        return carry

    lax.fori_loop(1, GROUP, step, 0)


def fold(block):
    half = block.shape[1] // 2
    return jnp.concatenate([block[:, :half], block[:, half:]], axis=0)


def unfold(block):
    return jnp.concatenate([block[:ROWS], block[ROWS:]], axis=1)


class Scatter:
    def __init__(self, axis, acc, refs):
        self.axis, self.acc = axis, acc
        self.psnd, self.prcv, self.gsnd, self.grcv, self.pss, self.prs, self.gss, self.grs = refs

    @staticmethod
    def scratch(chunks, width):
        return [
            pltpu.VMEM((chunks, GROUP * ROWS, width), BF16),
            pltpu.VMEM((chunks, GROUP * ROWS, width), BF16),
            pltpu.VMEM((chunks, GROUP, 2 * ROWS, width // 2), BF16),
            pltpu.VMEM((chunks, GROUP, 2 * ROWS, width // 2), BF16),
            pltpu.SemaphoreType.DMA((chunks,)),
            pltpu.SemaphoreType.DMA((chunks,)),
            pltpu.SemaphoreType.DMA((chunks, GROUP)),
            pltpu.SemaphoreType.DMA((chunks, GROUP)),
        ]

    def rows(self, q, g, pair):
        return self.acc[q, pl.ds(pl.multiple_of(g * 16 + pair * ROWS, ROWS), ROWS), :]

    def pair_copy(self, q):
        return remote(
            self.psnd.at[q], self.prcv.at[q], self.pss.at[q], self.prs.at[q], self.axis.partner()
        )

    def group_copy(self, q, k):
        return remote(
            self.gsnd.at[q, self.axis.peer_group(k)],
            self.grcv.at[q, k],
            self.gss.at[q, k],
            self.grs.at[q, k],
            self.axis.peer(k),
        )

    def send_pair(self, q):
        other = 1 - self.axis.pair
        for g in range(0, GROUP, 2):
            two = jnp.concatenate([self.rows(q, g, other), self.rows(q, g + 1, other)], axis=0)
            self.psnd[q, g * ROWS : (g + 2) * ROWS, :] = two.astype(BF16)
        self.pair_copy(q).start()

    def send_group(self, q):
        self.pair_copy(q).wait_recv()
        for g in range(0, GROUP, 2):
            came = self.prcv[q, g * ROWS : (g + 2) * ROWS, :].astype(F32)
            for i in range(2):
                both = self.rows(q, g + i, self.axis.pair) + came[i * ROWS : (i + 1) * ROWS]
                self.gsnd[q, g + i] = fold(both).astype(BF16)
        each_peer(lambda k: self.group_copy(q, k).start())

    def total(self, q):
        each_peer(lambda k: self.group_copy(q, k).wait_recv())
        total = self.gsnd[q, self.axis.group].astype(F32)
        for k in range(1, GROUP):
            total = total + self.grcv[q, k].astype(F32)
        return total

    def drain(self, q):
        self.pair_copy(q).wait_send()
        each_peer(lambda k: self.group_copy(q, k).wait_send())


class Gather:
    def __init__(self, axis, refs):
        self.axis = axis
        self.held, self.pss, self.prs, self.gss, self.grs = refs

    @staticmethod
    def scratch(chunks, width):
        return [
            pltpu.VMEM((chunks, 2, GROUP, 2 * ROWS, width // 2), BF16),
            pltpu.SemaphoreType.DMA((chunks,)),
            pltpu.SemaphoreType.DMA((chunks,)),
            pltpu.SemaphoreType.DMA((chunks, GROUP)),
            pltpu.SemaphoreType.DMA((chunks, GROUP)),
        ]

    def pair_copy(self, q):
        mine = self.held.at[q, self.axis.pair]
        return remote(mine, mine, self.pss.at[q], self.prs.at[q], self.axis.partner())

    def group_copy(self, q, k):
        mine = self.held.at[q, self.axis.pair, self.axis.group]
        return remote(mine, mine, self.gss.at[q, k], self.grs.at[q, k], self.axis.peer(k))

    def send_group(self, q, block):
        self.held[q, self.axis.pair, self.axis.group] = block.astype(BF16)
        each_peer(lambda k: self.group_copy(q, k).start())

    def send_pair(self, q):
        each_peer(lambda k: self.group_copy(q, k).wait_recv())
        self.pair_copy(q).start()

    def wait(self, q):
        self.pair_copy(q).wait_recv()

    def write_rows(self, q, out, width):
        half = width // 2
        for g in range(GROUP):
            even = self.held[q, 0, g].astype(F32)
            odd = self.held[q, 1, g].astype(F32)
            for side in range(2):
                rows = slice(side * ROWS, (side + 1) * ROWS)
                both = jnp.concatenate([even[rows], odd[rows]], axis=0)
                out[g * 16 : g * 16 + 16, side * half : (side + 1) * half] = both.astype(BF16)

    def drain(self, q):
        self.pair_copy(q).wait_send()
        each_peer(lambda k: self.group_copy(q, k).wait_send())


def staged(steps, stages):
    def body(t, carry):
        for start, run in stages:

            @pl.when((t >= start) & (t < start + CHUNKS))
            def _():
                run(t - start)

        return carry

    lax.fori_loop(0, steps, body, 0)


def kernel(n_scatter, n_gather, amps, integrals, vir, occ, one, two, three, *scratch):
    scratch = list(scratch)

    def take(n):
        out = scratch[:n]
        del scratch[:n]
        return out

    block, block_sem, vir_held, vir_sem, den_second, den_first, first, chunk = take(8)
    acc_one, acc_two, acc_three = take(3)
    size = block.shape[0]
    width = size // CHUNKS
    ab, cd = Axis("ab", "cd"), Axis("cd", "ab")
    scatter_one = Scatter(cd, acc_one, take(n_scatter))
    scatter_two = Scatter(ab, acc_two, take(n_scatter))
    scatter_three = Scatter(cd, acc_three, take(n_scatter))
    gather_one = Gather(ab, take(n_gather))
    gather_two = Gather(cd, take(n_gather))
    gather_three = Gather(ab, take(n_gather))

    def load(q):
        rows = pl.ds(pl.multiple_of(q * width, width), width)
        return pltpu.make_async_copy(integrals.at[rows, :], block.at[rows, :], block_sem.at[q])

    def load_vir(i, axis):
        rows = size // LANES
        return pltpu.make_async_copy(
            vir.at[pl.ds(pl.multiple_of(axis.index * rows, rows), rows), :], vir_held.at[i], vir_sem.at[i]
        )

    barrier = pltpu.get_barrier_semaphore()
    for axis in (ab, cd):
        each_peer(
            lambda k: pl.semaphore_signal(barrier, inc=1, device_id=axis.peer(k), device_id_type=MESH)
        )
        pl.semaphore_signal(barrier, inc=1, device_id=axis.partner(), device_id_type=MESH)
    load_vir(0, ab).start()
    load_vir(1, cd).start()
    for q in range(CHUNKS):
        load(q).start()
    mine = fold(amps[...].astype(F32))
    pl.semaphore_wait(barrier, 2 * GROUP)
    gather_one.send_group(0, mine)

    load_vir(0, ab).wait()
    load_vir(1, cd).wait()
    row = lax.broadcasted_iota(jnp.int32, (ROWS, LANES), 0)
    for i, axis, den in ((0, cd, den_second), (1, ab, den_first)):
        levels = jnp.zeros((ROWS, LANES), F32)
        for r in range(ROWS):
            levels = jnp.where(row == r, occ[axis.index * ROWS + r], levels)
        for tile in range(size // LANES):
            per_half = width // 2 // LANES
            q, side, at = tile // (2 * per_half), tile // per_half % 2, tile % per_half
            den[q, side * ROWS : (side + 1) * ROWS, at * LANES : (at + 1) * LANES] = (
                jnp.broadcast_to(vir_held[i, tile : tile + 1, :], (ROWS, LANES)) - levels
            )
    acc_two[...] = jnp.zeros_like(acc_two)
    acc_three[...] = jnp.zeros_like(acc_three)
    gather_one.send_pair(0)
    gather_one.wait(0)
    gather_one.write_rows(0, first, size)

    def columns(q):
        return pl.ds(pl.multiple_of(q * width, width), width)

    def product_one(n):
        load(n).wait()
        acc_one[n] = lax.dot_general(
            first[...], block[columns(n), :], (((1,), (1,)), ((), ())), preferred_element_type=F32
        )
        scatter_one.send_pair(n)

    def finish(scatter, out, den, gather, q):
        total = scatter.total(q)
        out[:, columns(q)] = unfold(total).astype(BF16)
        if gather is not None:
            gather.send_group(q, total / den[q])

    def product(gather, scatter, acc, over_rows, q):
        gather.wait(q)
        gather.write_rows(q, chunk, width)

        def part(n, carry):
            if over_rows:
                acc[n] += jnp.dot(
                    chunk[...], block[columns(q), columns(n)], preferred_element_type=F32
                )
            else:
                acc[n] += lax.dot_general(
                    chunk[...],
                    block[columns(n), columns(q)],
                    (((1,), (1,)), ((), ())),
                    preferred_element_type=F32,
                )

            @pl.when(q == CHUNKS - 1)
            def _():
                scatter.send_pair(n)

            return carry

        lax.fori_loop(0, CHUNKS, part, 0)

    s0, s1, s2, s3, s4 = STAGES
    staged(
        s4 + CHUNKS,
        (
            (s0, product_one),
            (s1, scatter_one.send_group),
            (s2, functools.partial(finish, scatter_one, one, den_second, gather_two)),
            (s3, gather_two.send_pair),
            (s4, functools.partial(product, gather_two, scatter_two, acc_two, True)),
        ),
    )
    staged(
        s4 - s1 + CHUNKS,
        (
            (0, scatter_two.send_group),
            (s2 - s1, functools.partial(finish, scatter_two, two, den_first, gather_three)),
            (s3 - s1, gather_three.send_pair),
            (s4 - s1, functools.partial(product, gather_three, scatter_three, acc_three, False)),
        ),
    )
    staged(
        s2 - s1 + CHUNKS,
        (
            (0, scatter_three.send_group),
            (s2 - s1, functools.partial(finish, scatter_three, three, None, None)),
        ),
    )

    gather_one.drain(0)

    def drain(q, carry):
        for part in (scatter_one, scatter_two, scatter_three, gather_two, gather_three):
            part.drain(q)
        return carry

    lax.fori_loop(0, CHUNKS, drain, 0)


def per_device(amplitudes, integrals, vir_energy, occ_energy):
    size = integrals.shape[0]
    width = size // CHUNKS
    rows = occ_energy.shape[0]
    scatter = Scatter.scratch(CHUNKS, width)
    gather = Gather.scratch(CHUNKS, width)
    vmem = pl.BlockSpec(memory_space=pltpu.VMEM)
    hbm = pl.BlockSpec(memory_space=pl.ANY)
    out = jax.ShapeDtypeStruct(amplitudes.shape, BF16)
    return pl.pallas_call(
        functools.partial(kernel, len(scatter), len(gather)),
        out_shape=(out, out, out),
        in_specs=[vmem, hbm, hbm, pl.BlockSpec(memory_space=pltpu.SMEM)],
        out_specs=(vmem, vmem, vmem),
        scratch_shapes=[
            pltpu.VMEM((size, size), BF16),
            pltpu.SemaphoreType.DMA((CHUNKS,)),
            pltpu.VMEM((2, size // LANES, LANES), F32),
            pltpu.SemaphoreType.DMA((2,)),
            pltpu.VMEM((CHUNKS, 2 * ROWS, width // 2), F32),
            pltpu.VMEM((CHUNKS, 2 * ROWS, width // 2), F32),
            pltpu.VMEM((rows, size), BF16),
            pltpu.VMEM((rows, width), BF16),
        ]
        + [pltpu.VMEM((CHUNKS, rows, width), F32)] * 3
        + scatter * 3
        + Gather.scratch(1, size)
        + gather * 2,
        compiler_params=pltpu.CompilerParams(
            collective_id=0, has_side_effects=True, vmem_limit_bytes=40 * 2**20
        ),
        cost_estimate=pl.CostEstimate(
            flops=6 * rows * size * size, bytes_accessed=2 * size * size, transcendentals=0
        ),
        name="ladder",
    )(amplitudes, integrals, vir_energy.reshape(-1, LANES), occ_energy)


def solution(mesh):
    return jax.shard_map(
        per_device,
        mesh=mesh,
        in_specs=(P("ab", "cd"), P("ab", "cd"), P(), P()),
        out_specs=(P("cd", "ab"), P("ab", "cd"), P("cd", "ab")),
        check_vma=False,
    )
```

time: 586 us -> 86.4 us (0.15)
  waiting for transfers between devices: 463 us -> 0 us
  blocking collectives: 84 us -> 0 us
  Pallas kernels: 0 us -> 76.9 us
  matrix products: 20 us -> 0 us
  between operations: 13.8 us -> 0.65 us
  local copies, waits for them, and re-layouts: 0.8 us -> 7.54 us
    reduce_scatter x3 -> x0, waiting for transfers between devices: 463 us -> none  [the longest x2 409 us: scatter_cd(): lax.psum_scatter(lax.dot_general(gathered, integrals, (((1,), (1,)), ((),...]
    all_gather x3 -> x0, blocking collectives: 84 us -> none  [the longest x2 42.9 us: gather_ab(): return lax.all_gather(amps, 'ab', axis=0, tiled=True)]
    pallas_call x0 -> x1, Pallas kernels: none -> 76.9 us  [per_device(): pl.pallas_call(functools.partial(kernel, len(scatter), len(gather)), out_...]
    dot_general x3 -> x0, matrix products: 20 us -> none  [the longest x2 14.5 us: scatter_cd(): lax.dot_general(gathered, integrals, (((1,), (1,)), ((), ())), preferred_...]
    unnamed x2 -> x11, local copies, waits for them, and re-layouts: 0.01 us -> 7.54 us
  transfers between devices with their start and end apart: 3 -> 0, of which waited for: 3 -> 0; matrix products, arithmetic and copies ran while one was open for 0% -> 0% of each run, Pallas kernels for 0% -> 0%
where the time goes in v1:
time: 86.4 us; the launch traced here: 85.1 us
  Pallas kernels  76.9 us (89%)
  local copies, waits for them, and re-layouts  7.54 us (9%)
    pallas_call x1, Pallas kernels, per_device(): pl.pallas_call(functools.partial(kernel, len(scatter), len(gather)), out_...  76.9 us
    unnamed x11, local copies, waits for them, and re-layouts  7.54 us

profile of v1, /device:TPU:8, one launch (start us, length us, event | category | flops | bytes accessed | tf_op | source)
XLA Modules:
  0.0 85.1 jit_solution(10033822116353540575)
XLA Ops:
  0.6 0.0 copy-start
  0.6 3.4 %copy-done = bf16[2048,2048]{1,0:T(8,128)(2,1)S(1)} copy-done((bf16[2048,2048]{1,0:T(8,128)(2,1)S(1)}, bf16[2048,2048]{1,0:T(8,128)(2,1)}, u32[]{:S(2)}) %copy-start) | copy-done | bytes 8388632
  4.0 0.0 copy-start.1
  4.0 0.9 %copy-done.1 = f32[32768]{0:T(1024)S(1)} copy-done((f32[32768]{0:T(1024)S(1)}, f32[32768]{0:T(1024)}, u32[]{:S(2)}) %copy-start.1) | copy-done | bytes 131096
  4.9 0.0 copy-start.2
  4.9 0.8 copy-done.2
  5.7 0.0 copy-start.3
  5.7 0.7 copy-done.3
  6.3 76.9 %ladder.1 = (bf16[8,2048]{1,0:T(8,128)(2,1)S(1)}, bf16[8,2048]{1,0:T(8,128)(2,1)S(1)}, bf16[8,2048]{1,0:T(8,128)(2,1)S(1)}) custom-call(bf16[8,2048]{1,0:T(8,128)(2,1)S(1)} %copy-done.2, bf16[2048,2048]{1,0:T(8,128)(2,1)S(1)} %copy-done, f32[256,128]{1,0:T(8,128)S(1)} %bitcast.1, f32[128]{0:T(128)S(1)} %copy-done.3), custom_call_target="tpu_custom_call" | custom-call | flops 3221225472 | bytes 8388608 | tf_op jit(solution)/shard_map/ladder/pallas_call | solution.py:344
  83.3 0.6 copy.10
  83.9 0.6 copy.11
  84.5 0.6 copy.12
Async XLA Ops:
  0.6 3.4 %copy-start = (bf16[2048,2048]{1,0:T(8,128)(2,1)S(1)}, bf16[2048,2048]{1,0:T(8,128)(2,1)}, u32[]{:S(2)}) copy-start(bf16[2048,2048]{1,0:T(8,128)(2,1)} %integrals.1) | copy-start | bytes 25165828
  4.0 0.9 %copy-start.1 = (f32[32768]{0:T(1024)S(1)}, f32[32768]{0:T(1024)}, u32[]{:S(2)}) copy-start(f32[32768]{0:T(1024)} %param.6) | copy-start | bytes 393220
  4.9 0.8 copy-start.2
  5.7 0.7 copy-start.3

commit v2 on v1

v2 whole, which is shorter than its diff:
```python
import functools

import jax
import jax.numpy as jnp
from jax import lax
from jax.experimental import pallas as pl
from jax.experimental.pallas import tpu as pltpu
from jax.sharding import PartitionSpec as P

MESH = pl.DeviceIdType.MESH
F32 = jnp.float32
BF16 = jnp.bfloat16

GROUP = 8
LANES = 128
ROWS = 8
CHUNKS = 4
TILE = 512
FAR_FIRST = (4, 3, 5, 2, 6, 1, 7)
VMEM_LIMIT = 60 * 2**20
STAGES_ONE = (0, 4, 7, 10, 13)
STAGES_TWO = (0, 3, 6, 9)
STAGES_THREE = (0, 3)
EARLY = 2


class Axis:
    def __init__(self, name, other):
        self.name = name
        self.index = lax.axis_index(name)
        self.other = lax.axis_index(other)
        self.group = lax.div(self.index, 2)
        self.pair = lax.rem(self.index, 2)
        self.groups = [lax.rem(self.group + k, GROUP) for k in range(GROUP)]
        self.peers = [self.device(g * 2 + self.pair) for g in self.groups]

    def device(self, index):
        return (index, self.other) if self.name == "ab" else (self.other, index)

    def peer_group(self, k):
        return self.groups[k]

    def peer(self, k):
        return self.peers[k]

    def partner(self):
        return self.device(self.group * 2 + 1 - self.pair)


def remote(src, dst, send, recv, device):
    return pltpu.make_async_remote_copy(
        src_ref=src, dst_ref=dst, send_sem=send, recv_sem=recv, device_id=device, device_id_type=MESH
    )


def each_peer(body):
    for k in FAR_FIRST:
        body(k)


def wait_bytes(ref, sem):
    pltpu.make_async_copy(ref, ref, sem).wait()


def fold(block):
    half = block.shape[1] // 2
    return jnp.concatenate([block[:, :half], block[:, half:]], axis=0)


def unfold(block):
    return jnp.concatenate([block[:ROWS], block[ROWS:]], axis=1)


class Scatter:
    def __init__(self, axis, acc, refs):
        self.axis, self.acc = axis, acc
        self.psnd, self.prcv, self.gsnd, self.grcv, self.sent, self.came = refs

    @staticmethod
    def scratch(chunks, width):
        return [
            pltpu.VMEM((chunks, GROUP * ROWS, width), BF16),
            pltpu.VMEM((chunks, GROUP * ROWS, width), BF16),
            pltpu.VMEM((chunks, GROUP, 2 * ROWS, width // 2), BF16),
            pltpu.VMEM((chunks, GROUP - 1, 2 * ROWS, width // 2), BF16),
            pltpu.SemaphoreType.DMA((2,)),
            pltpu.SemaphoreType.DMA((2, chunks)),
        ]

    def rows(self, q, g, pair):
        width = self.psnd.shape[-1]
        return self.acc[
            pl.ds(pl.multiple_of(g * 16 + pair * ROWS, ROWS), ROWS),
            pl.ds(pl.multiple_of(q * width, width), width),
        ]

    def pair_copy(self, q):
        return remote(
            self.psnd.at[q], self.prcv.at[q], self.sent.at[0], self.came.at[0, q], self.axis.partner()
        )

    def group_copy(self, q, k):
        return remote(
            self.gsnd.at[q, self.axis.peer_group(k)],
            self.grcv.at[q, k - 1],
            self.sent.at[1],
            self.came.at[1, q],
            self.axis.peer(k),
        )

    def send_pair(self, q):
        other = 1 - self.axis.pair
        for g in range(0, GROUP, 2):
            two = jnp.concatenate([self.rows(q, g, other), self.rows(q, g + 1, other)], axis=0)
            self.psnd[q, g * ROWS : (g + 2) * ROWS, :] = two.astype(BF16)
        self.pair_copy(q).start()

    def send_group(self, q):
        wait_bytes(self.prcv.at[q], self.came.at[0, q])
        for g in range(0, GROUP, 2):
            came = self.prcv[q, g * ROWS : (g + 2) * ROWS, :].astype(F32)
            for i in range(2):
                both = self.rows(q, g + i, self.axis.pair) + came[i * ROWS : (i + 1) * ROWS]
                self.gsnd[q, g + i] = fold(both).astype(BF16)
        each_peer(lambda k: self.group_copy(q, k).start())

    def total(self, q):
        wait_bytes(self.grcv.at[q], self.came.at[1, q])
        total = self.gsnd[q, self.axis.group].astype(F32)
        for k in range(GROUP - 1):
            total = total + self.grcv[q, k].astype(F32)
        return total

    def drain(self, pairs=True, groups=True):
        if pairs:
            wait_bytes(self.psnd, self.sent.at[0])
        if groups:
            wait_bytes(self.grcv, self.sent.at[1])


class Gather:
    def __init__(self, axis, refs):
        self.axis = axis
        self.held, self.sent, self.came = refs

    @staticmethod
    def scratch(chunks, width):
        return [
            pltpu.VMEM((chunks, 2, GROUP, 2 * ROWS, width // 2), BF16),
            pltpu.SemaphoreType.DMA((2,)),
            pltpu.SemaphoreType.DMA((2, chunks)),
        ]

    def pair_copy(self, q):
        mine = self.held.at[q, self.axis.pair]
        return remote(mine, mine, self.sent.at[0], self.came.at[0, q], self.axis.partner())

    def group_copy(self, q, k):
        mine = self.held.at[q, self.axis.pair, self.axis.group]
        return remote(mine, mine, self.sent.at[1], self.came.at[1, q], self.axis.peer(k))

    def send_group(self, q, block):
        self.held[q, self.axis.pair, self.axis.group] = block.astype(BF16)
        each_peer(lambda k: self.group_copy(q, k).start())

    def send_pair(self, q):
        wait_bytes(self.held.at[q, 0, pl.ds(0, GROUP - 1)], self.came.at[1, q])
        self.pair_copy(q).start()

    def wait(self, q):
        wait_bytes(self.held.at[q, 0], self.came.at[0, q])

    def write_rows(self, q, out, start):
        half = self.held.shape[-1]
        for g in range(GROUP):
            even = self.held[q, 0, g].astype(F32)
            odd = self.held[q, 1, g].astype(F32)
            for side in range(2):
                rows = slice(side * ROWS, (side + 1) * ROWS)
                both = jnp.concatenate([even[rows], odd[rows]], axis=0)
                at = start + side * half
                out[g * 16 : g * 16 + 16, at : at + half] = both.astype(BF16)

    def drain(self):
        wait_bytes(self.held.at[:, 0], self.sent.at[0])
        wait_bytes(self.held.at[:, 0, pl.ds(0, GROUP - 1)], self.sent.at[1])


def staged(steps, stages):
    def body(t, carry):
        for start, run in stages:

            @pl.when((t >= start) & (t < start + CHUNKS))
            def _():
                run(t - start)

        return carry

    lax.fori_loop(0, steps, body, 0)


def kernel(n_scatter, n_gather, amps, integrals, vir, occ, one, two, three, *scratch):
    outs = one, two, three
    scratch = list(scratch)

    def take(n):
        out = scratch[:n]
        del scratch[:n]
        return out

    amps_held, occ_held, block, block_sem, vir_held, vir_sem, den_second, den_first, first, chunk, out_held, out_sem = take(12)
    acc_one, acc_two, acc_three = take(3)
    size = block.shape[0]
    width = size // CHUNKS
    tiles, per_tile = size // TILE, TILE // width
    ab, cd = Axis("ab", "cd"), Axis("cd", "ab")
    scatter_one = Scatter(cd, acc_one, take(n_scatter))
    scatter_two = Scatter(ab, acc_two, take(n_scatter))
    scatter_three = Scatter(cd, acc_three, take(n_scatter))
    gather_one = Gather(ab, take(n_gather))
    gather_two = Gather(cd, take(n_gather))
    gather_three = Gather(ab, take(n_gather))

    def load(q):
        rows = pl.ds(pl.multiple_of(q * TILE, TILE), TILE)
        return pltpu.make_async_copy(integrals.at[rows, :], block.at[rows, :], block_sem.at[q])

    def load_vir(i, axis):
        rows = size // LANES
        return pltpu.make_async_copy(
            vir.at[pl.ds(pl.multiple_of(axis.index * rows, rows), rows), :], vir_held.at[i], vir_sem.at[i]
        )

    load_amps = pltpu.make_async_copy(amps, amps_held, vir_sem.at[2])
    load_occ = pltpu.make_async_copy(occ, occ_held, vir_sem.at[3])

    barrier = pltpu.get_barrier_semaphore()
    for axis in (ab, cd):
        each_peer(
            lambda k: pl.semaphore_signal(barrier, inc=1, device_id=axis.peer(k), device_id_type=MESH)
        )
        pl.semaphore_signal(barrier, inc=1, device_id=axis.partner(), device_id_type=MESH)
    load_amps.start()
    load_vir(0, ab).start()
    load_vir(1, cd).start()
    load_occ.start()
    for q in range(EARLY):
        load(q).start()
    load_amps.wait()
    mine = fold(amps_held[...].astype(F32))
    pl.semaphore_wait(barrier, 2 * GROUP)
    gather_one.send_group(0, mine)
    for q in range(EARLY, tiles):
        load(q).start()

    load_vir(0, ab).wait()
    load_vir(1, cd).wait()
    load_occ.wait()
    row = lax.broadcasted_iota(jnp.int32, (ROWS, LANES), 0)
    for i, axis, den in ((0, cd, den_second), (1, ab, den_first)):
        levels = jnp.zeros((ROWS, LANES), F32)
        for r in range(ROWS):
            levels = jnp.where(row == r, occ_held[axis.index * ROWS + r], levels)
        for lane_tile in range(size // LANES):
            per_half = width // 2 // LANES
            part = lane_tile // per_half
            q, side, at = part // 2, part % 2, lane_tile % per_half
            den[q, side * ROWS : (side + 1) * ROWS, at * LANES : (at + 1) * LANES] = (
                jnp.broadcast_to(vir_held[i, lane_tile : lane_tile + 1, :], (ROWS, LANES)) - levels
            )
    acc_two[...] = jnp.zeros_like(acc_two)
    acc_three[...] = jnp.zeros_like(acc_three)
    gather_one.send_pair(0)
    gather_one.wait(0)
    gather_one.write_rows(0, first, 0)

    def columns(q):
        return pl.ds(pl.multiple_of(q * width, width), width)

    def tile(n):
        return pl.ds(pl.multiple_of(n * TILE, TILE), TILE)

    def product_one(q):
        @pl.when(lax.rem(q, per_tile) == 0)
        def _():
            n = lax.div(q, per_tile)
            load(n).wait()
            acc_one[:, tile(n)] = lax.dot_general(
                first[...], block[tile(n), :], (((1,), (1,)), ((), ())), preferred_element_type=F32
            )
            for i in range(per_tile):
                scatter_one.send_pair(q + i)

    def store(i):
        return pltpu.make_async_copy(out_held.at[i], outs[i], out_sem.at[i])

    def finish(scatter, i, den, gather, q):
        total = scatter.total(q)
        if gather is not None:
            gather.send_group(q, total / den[q])
        out_held[i, :, columns(q)] = unfold(total).astype(BF16)

        @pl.when(q == CHUNKS - 1)
        def _():
            store(i).start()

    def product(gather, scatter, acc, over_rows, q):
        gather.wait(q)
        for i in range(per_tile):

            @pl.when(lax.rem(q, per_tile) == i)
            def _():
                gather.write_rows(q, chunk, i * width)

        @pl.when(lax.rem(q, per_tile) == per_tile - 1)
        def _():
            m = lax.div(q, per_tile)

            def part(n, carry):
                if over_rows:
                    acc[:, tile(n)] += jnp.dot(
                        chunk[...], block[tile(m), tile(n)], preferred_element_type=F32
                    )
                else:
                    acc[:, tile(n)] += lax.dot_general(
                        chunk[...],
                        block[tile(n), tile(m)],
                        (((1,), (1,)), ((), ())),
                        preferred_element_type=F32,
                    )

                @pl.when(q == CHUNKS - 1)
                def _():
                    for i in range(per_tile):
                        scatter.send_pair(n * per_tile + i)

                return carry

            lax.fori_loop(0, tiles, part, 0)

    s0, s1, s2, s3, s4 = STAGES_ONE
    staged(
        s4 + CHUNKS,
        (
            (s0, product_one),
            (s1, scatter_one.send_group),
            (s2, functools.partial(finish, scatter_one, 0, den_second, gather_two)),
            (s3, gather_two.send_pair),
            (s4, functools.partial(product, gather_two, scatter_two, acc_two, True)),
        ),
    )
    s0, s1, s2, s3 = STAGES_TWO
    staged(
        s3 + CHUNKS,
        (
            (s0, scatter_two.send_group),
            (s1, functools.partial(finish, scatter_two, 1, den_first, gather_three)),
            (s2, gather_three.send_pair),
            (s3, functools.partial(product, gather_three, scatter_three, acc_three, False)),
        ),
    )
    s0, s1 = STAGES_THREE
    staged(
        s1 + CHUNKS,
        (
            (s0, scatter_three.send_group),
            (s1, functools.partial(finish, scatter_three, 2, None, None)),
        ),
    )

    for part in (gather_one, gather_two, gather_three, scatter_one, scatter_two, scatter_three):
        part.drain()
    for i in range(3):
        store(i).wait()


def hand_on(*refs):
    sources, targets, held, sems = refs[:3], refs[3:6], refs[6], refs[7]
    came = [pltpu.make_async_copy(sources[i], held.at[i], sems.at[i]) for i in range(3)]
    gone = [pltpu.make_async_copy(held.at[i], targets[i], sems.at[i]) for i in range(3)]
    for copy in came:
        copy.start()
    for i in range(3):
        came[i].wait()
        gone[i].start()
    for copy in gone:
        copy.wait()


def per_device(amplitudes, integrals, vir_energy, occ_energy):
    size = integrals.shape[0]
    width = size // CHUNKS
    rows = occ_energy.shape[0]
    scatter = Scatter.scratch(CHUNKS, width)
    gather = Gather.scratch(CHUNKS, width)
    hbm = pl.BlockSpec(memory_space=pltpu.HBM)
    out = jax.ShapeDtypeStruct(amplitudes.shape, BF16)
    ladders = pl.pallas_call(
        functools.partial(kernel, len(scatter), len(gather)),
        out_shape=(out, out, out),
        in_specs=[hbm] * 4,
        out_specs=(hbm, hbm, hbm),
        scratch_shapes=[
            pltpu.VMEM(amplitudes.shape, BF16),
            pltpu.SMEM((rows,), F32),
            pltpu.VMEM((size, size), BF16),
            pltpu.SemaphoreType.DMA((size // TILE,)),
            pltpu.VMEM((2, size // LANES, LANES), F32),
            pltpu.SemaphoreType.DMA((4,)),
            pltpu.VMEM((CHUNKS, 2 * ROWS, width // 2), F32),
            pltpu.VMEM((CHUNKS, 2 * ROWS, width // 2), F32),
            pltpu.VMEM((rows, size), BF16),
            pltpu.VMEM((rows, TILE), BF16),
            pltpu.VMEM((3,) + amplitudes.shape, BF16),
            pltpu.SemaphoreType.DMA((3,)),
        ]
        + [pltpu.VMEM((rows, size), F32)] * 3
        + scatter * 3
        + Gather.scratch(1, size)
        + gather * 2,
        compiler_params=pltpu.CompilerParams(
            collective_id=0, has_side_effects=True, vmem_limit_bytes=VMEM_LIMIT
        ),
        cost_estimate=pl.CostEstimate(
            flops=6 * rows * size * size, bytes_accessed=2 * size * size, transcendentals=0
        ),
        name="ladder",
    )(amplitudes, integrals, vir_energy.reshape(-1, LANES), occ_energy)
    return pl.pallas_call(
        hand_on,
        out_shape=(out, out, out),
        in_specs=[hbm] * 3,
        out_specs=(hbm,) * 3,
        scratch_shapes=[pltpu.VMEM((3,) + amplitudes.shape, BF16), pltpu.SemaphoreType.DMA((3,))],
        name="hand_on",
    )(*ladders)


def solution(mesh):
    return jax.shard_map(
        per_device,
        mesh=mesh,
        in_specs=(P("ab", "cd"), P("ab", "cd"), P(), P()),
        out_specs=(P("cd", "ab"), P("ab", "cd"), P("cd", "ab")),
        check_vma=False,
    )
```

time: 86.4 us -> 70 us (0.81); the launches traced: 85.1 us -> 69.8 us
  Pallas kernels: 76.9 us -> 69.2 us
  local copies, waits for them, and re-layouts: 7.54 us -> 0 us
    pallas_call x1, Pallas kernels: 76.9 us -> 67.7 us  [per_device(): pl.pallas_call(functools.partial(kernel, len(scatter), len(gather)), out_...]
    unnamed x11 -> x0, local copies, waits for them, and re-layouts: 7.54 us -> none
    pallas_call x0 -> x1, Pallas kernels: none -> 1.43 us  [per_device(): pl.pallas_call(hand_on, out_shape=(out, out, out), in_specs=[hbm] * 3, ou...]
where the time goes in v2:
time: 70 us; the launch traced here: 69.8 us
  Pallas kernels  69.2 us (99%)
    pallas_call x1, Pallas kernels, per_device(): pl.pallas_call(functools.partial(kernel, len(scatter), len(gather)), out_...  67.7 us
    pallas_call x1, Pallas kernels, per_device(): pl.pallas_call(hand_on, out_shape=(out, out, out), in_specs=[hbm] * 3, ou...  1.43 us

profile of v2, /device:TPU:8, one launch (start us, length us, event | category | flops | bytes accessed | tf_op | source)
XLA Modules:
  0.0 69.8 jit_solution(14578813024768958093)
XLA Ops:
  0.6 67.7 %ladder.1 = (bf16[8,2048]{1,0:T(8,128)(2,1)}, bf16[8,2048]{1,0:T(8,128)(2,1)}, bf16[8,2048]{1,0:T(8,128)(2,1)}) custom-call(bf16[8,2048]{1,0:T(8,128)(2,1)} %amps.1, bf16[2048,2048]{1,0:T(8,128)(2,1)} %integrals.1, f32[256,128]{1,0:T(8,128)} %bitcast.1, f32[128]{0:T(128)} %occ.1), custom_call_target="tpu_custom_call" | custom-call | flops 3221225472 | bytes 8388608 | tf_op jit(solution)/shard_map/ladder/pallas_call | solution.py:398
  68.4 1.4 %hand_on.1 = (bf16[8,2048]{1,0:T(8,128)(2,1)}, bf16[8,2048]{1,0:T(8,128)(2,1)}, bf16[8,2048]{1,0:T(8,128)(2,1)}) custom-call(bf16[8,2048]{1,0:T(8,128)(2,1)} %get-tuple-element.6.refs_0_, bf16[8,2048]{1,0:T(8,128)(2,1)} %get-tuple-element.7.refs_1_, bf16[8,2048]{1,0:T(8,128)(2,1)} %get-tuple-element.8.refs_2_), custom_call_target="tpu_custom_call" | custom-call | tf_op jit(solution)/shard_map/hand_on/pallas_call | solution.py:429

commit v3 on v2

--- a/solution.py
+++ b/solution.py
@@ -20,8 +20,10 @@
 VMEM_LIMIT = 60 * 2**20
 STAGES_ONE = (0, 4, 7, 10, 13)
 STAGES_TWO = (0, 3, 6, 9)
-STAGES_THREE = (0, 3)
-EARLY = 2
+STAGES_THREE = (0, 4)
+AMP_CHUNKS = 1
+WIDE_ONE = (2,)
+WIDE_THREE = (3,)
 
 
 class Axis:
@@ -37,12 +39,6 @@
     def device(self, index):
         return (index, self.other) if self.name == "ab" else (self.other, index)
 
-    def peer_group(self, k):
-        return self.groups[k]
-
-    def peer(self, k):
-        return self.peers[k]
-
     def partner(self):
         return self.device(self.group * 2 + 1 - self.pair)
 
@@ -58,6 +54,10 @@
         body(k)
 
 
+def dot(left, right):
+    return jnp.dot(left, right, preferred_element_type=F32)
+
+
 def wait_bytes(ref, sem):
     pltpu.make_async_copy(ref, ref, sem).wait()
 
@@ -72,13 +72,16 @@
 
 
 class Scatter:
-    def __init__(self, axis, acc, refs):
-        self.axis, self.acc = axis, acc
-        self.psnd, self.prcv, self.gsnd, self.grcv, self.sent, self.came = refs
+    def __init__(self, axis, acc, wide, refs):
+        self.axis, self.acc, self.wide = axis, acc, wide
+        self.psnd, self.prcv, self.gsnd, self.grcv, self.sent, self.came = refs[:6]
+        if wide:
+            self.wsnd, self.wrcv, self.wpsnd, self.wprcv, self.wsum, self.wsent, self.wcame = refs[6:]
+        self.width = self.psnd.shape[-1]
 
     @staticmethod
-    def scratch(chunks, width):
-        return [
+    def scratch(chunks, width, wide):
+        out = [
             pltpu.VMEM((chunks, GROUP * ROWS, width), BF16),
             pltpu.VMEM((chunks, GROUP * ROWS, width), BF16),
             pltpu.VMEM((chunks, GROUP, 2 * ROWS, width // 2), BF16),
@@ -86,13 +89,35 @@
             pltpu.SemaphoreType.DMA((2,)),
             pltpu.SemaphoreType.DMA((2, chunks)),
         ]
+        if wide:
+            n = len(wide)
+            out += [
+                pltpu.VMEM((n, GROUP, 2 * ROWS, width), BF16),
+                pltpu.VMEM((n, GROUP - 1, 2 * ROWS, width), BF16),
+                pltpu.VMEM((n, 2 * ROWS, width // 2), BF16),
+                pltpu.VMEM((n, 2 * ROWS, width // 2), BF16),
+                pltpu.VMEM((n, 2 * ROWS, width // 2), F32),
+                pltpu.SemaphoreType.DMA((2,)),
+                pltpu.SemaphoreType.DMA((2, n)),
+            ]
+        return out
+
+    def columns(self, q):
+        return pl.ds(pl.multiple_of(q * self.width, self.width), self.width)
 
     def rows(self, q, g, pair):
-        width = self.psnd.shape[-1]
-        return self.acc[
-            pl.ds(pl.multiple_of(g * 16 + pair * ROWS, ROWS), ROWS),
-            pl.ds(pl.multiple_of(q * width, width), width),
-        ]
+        at = pl.ds(pl.multiple_of(g * 16 + pair * ROWS, ROWS), ROWS)
+        return self.acc[at, self.columns(q)]
+
+    def either(self, q, narrow, wide):
+        is_wide = False
+        for i, w in enumerate(self.wide):
+            pl.when(q == w)(functools.partial(wide, i))
+            is_wide = (q == w) | is_wide
+        if self.wide:
+            pl.when(jnp.logical_not(is_wide))(narrow)
+        else:
+            narrow()
 
     def pair_copy(self, q):
         return remote(
@@ -101,41 +126,92 @@
 
     def group_copy(self, q, k):
         return remote(
-            self.gsnd.at[q, self.axis.peer_group(k)],
+            self.gsnd.at[q, self.axis.groups[k]],
             self.grcv.at[q, k - 1],
             self.sent.at[1],
             self.came.at[1, q],
-            self.axis.peer(k),
+            self.axis.peers[k],
         )
 
-    def send_pair(self, q):
-        other = 1 - self.axis.pair
-        for g in range(0, GROUP, 2):
-            two = jnp.concatenate([self.rows(q, g, other), self.rows(q, g + 1, other)], axis=0)
-            self.psnd[q, g * ROWS : (g + 2) * ROWS, :] = two.astype(BF16)
-        self.pair_copy(q).start()
-
-    def send_group(self, q):
-        wait_bytes(self.prcv.at[q], self.came.at[0, q])
-        for g in range(0, GROUP, 2):
-            came = self.prcv[q, g * ROWS : (g + 2) * ROWS, :].astype(F32)
-            for i in range(2):
-                both = self.rows(q, g + i, self.axis.pair) + came[i * ROWS : (i + 1) * ROWS]
-                self.gsnd[q, g + i] = fold(both).astype(BF16)
-        each_peer(lambda k: self.group_copy(q, k).start())
-
-    def total(self, q):
-        wait_bytes(self.grcv.at[q], self.came.at[1, q])
-        total = self.gsnd[q, self.axis.group].astype(F32)
-        for k in range(GROUP - 1):
-            total = total + self.grcv[q, k].astype(F32)
-        return total
-
-    def drain(self, pairs=True, groups=True):
-        if pairs:
-            wait_bytes(self.psnd, self.sent.at[0])
-        if groups:
-            wait_bytes(self.grcv, self.sent.at[1])
+    def wide_group_copy(self, i, k):
+        return remote(
+            self.wsnd.at[i, self.axis.groups[k]],
+            self.wrcv.at[i, k - 1],
+            self.wsent.at[0],
+            self.wcame.at[0, i],
+            self.axis.peers[k],
+        )
+
+    def wide_pair_copy(self, i):
+        return remote(
+            self.wpsnd.at[i], self.wprcv.at[i], self.wsent.at[1], self.wcame.at[1, i], self.axis.partner()
+        )
+
+    def begin(self, q):
+        def narrow():
+            other = 1 - self.axis.pair
+            for g in range(0, GROUP, 2):
+                two = jnp.concatenate([self.rows(q, g, other), self.rows(q, g + 1, other)], axis=0)
+                self.psnd[q, g * ROWS : (g + 2) * ROWS, :] = two.astype(BF16)
+            self.pair_copy(q).start()
+
+        def wide(i):
+            def send(k):
+                g = self.axis.groups[k]
+                both = pl.ds(pl.multiple_of(g * 16, 16), 16)
+                self.wsnd[i, g] = self.acc[both, self.columns(q)].astype(BF16)
+                if k:
+                    self.wide_group_copy(i, k).start()
+
+            each_peer(send)
+            send(0)
+
+        self.either(q, narrow, wide)
+
+    def middle(self, q):
+        def narrow():
+            wait_bytes(self.prcv.at[q], self.came.at[0, q])
+            for g in range(0, GROUP, 2):
+                came = self.prcv[q, g * ROWS : (g + 2) * ROWS, :].astype(F32)
+                for i in range(2):
+                    both = self.rows(q, g + i, self.axis.pair) + came[i * ROWS : (i + 1) * ROWS]
+                    self.gsnd[q, g + i] = fold(both).astype(BF16)
+            each_peer(lambda k: self.group_copy(q, k).start())
+
+        def wide(i):
+            wait_bytes(self.wrcv.at[i], self.wcame.at[0, i])
+            total = self.wsnd[i, self.axis.group].astype(F32)
+            for k in range(GROUP - 1):
+                total = total + self.wrcv[i, k].astype(F32)
+            even, odd = fold(total[:ROWS]), fold(total[ROWS:])
+            is_even = self.axis.pair == 0
+            self.wpsnd[i] = jnp.where(is_even, odd, even).astype(BF16)
+            self.wsum[i] = jnp.where(is_even, even, odd)
+            self.wide_pair_copy(i).start()
+
+        self.either(q, narrow, wide)
+
+    def end(self, q, use):
+        def narrow():
+            wait_bytes(self.grcv.at[q], self.came.at[1, q])
+            total = self.gsnd[q, self.axis.group].astype(F32)
+            for k in range(GROUP - 1):
+                total = total + self.grcv[q, k].astype(F32)
+            use(total)
+
+        def wide(i):
+            wait_bytes(self.wprcv.at[i], self.wcame.at[1, i])
+            use(self.wsum[i] + self.wprcv[i].astype(F32))
+
+        self.either(q, narrow, wide)
+
+    def drain(self):
+        count = self.psnd.shape[0] - len(self.wide)
+        wait_bytes(self.psnd.at[pl.ds(0, count)], self.sent.at[0])
+        wait_bytes(self.grcv.at[pl.ds(0, count)], self.sent.at[1])
+        if self.wide:
+            wait_bytes(self.wrcv, self.wsent.at[0])
+            wait_bytes(self.wpsnd, self.wsent.at[1])
 
 
 class Gather:
@@ -157,7 +233,7 @@
 
     def group_copy(self, q, k):
         mine = self.held.at[q, self.axis.pair, self.axis.group]
-        return remote(mine, mine, self.sent.at[1], self.came.at[1, q], self.axis.peer(k))
+        return remote(mine, mine, self.sent.at[1], self.came.at[1, q], self.axis.peers[k])
 
     def send_group(self, q, block):
         self.held[q, self.axis.pair, self.axis.group] = block.astype(BF16)
@@ -199,7 +275,7 @@
     lax.fori_loop(0, steps, body, 0)
 
 
-def kernel(n_scatter, n_gather, amps, integrals, vir, occ, one, two, three, *scratch):
+def kernel(amps, integrals, vir, occ, one, two, three, *scratch):
     outs = one, two, three
     scratch = list(scratch)
 
@@ -208,18 +284,18 @@
         del scratch[:n]
         return out
 
-    amps_held, occ_held, block, block_sem, vir_held, vir_sem, den_second, den_first, first, chunk, out_held, out_sem = take(12)
+    amps_held, occ_held, block, turned, block_sem, vir_held, vir_sem, den_second, den_first, first, chunk, out_held, out_sem = take(13)
     acc_one, acc_two, acc_three = take(3)
-    size = block.shape[0]
+    rows, size = first.shape
     width = size // CHUNKS
     tiles, per_tile = size // TILE, TILE // width
     ab, cd = Axis("ab", "cd"), Axis("cd", "ab")
-    scatter_one = Scatter(cd, acc_one, take(n_scatter))
-    scatter_two = Scatter(ab, acc_two, take(n_scatter))
-    scatter_three = Scatter(cd, acc_three, take(n_scatter))
-    gather_one = Gather(ab, take(n_gather))
-    gather_two = Gather(cd, take(n_gather))
-    gather_three = Gather(ab, take(n_gather))
+    scatter_one = Scatter(cd, acc_one, WIDE_ONE, take(13 if WIDE_ONE else 6))
+    scatter_two = Scatter(ab, acc_two, (), take(6))
+    scatter_three = Scatter(cd, acc_three, WIDE_THREE, take(13 if WIDE_THREE else 6))
+    gather_one = Gather(ab, take(3))
+    gather_two = Gather(cd, take(3))
+    gather_three = Gather(ab, take(3))
 
     def load(q):
         rows = pl.ds(pl.multiple_of(q * TILE, TILE), TILE)
@@ -237,21 +313,21 @@
     barrier = pltpu.get_barrier_semaphore()
     for axis in (ab, cd):
         each_peer(
-            lambda k: pl.semaphore_signal(barrier, inc=1, device_id=axis.peer(k), device_id_type=MESH)
+            lambda k: pl.semaphore_signal(barrier, inc=1, device_id=axis.peers[k], device_id_type=MESH)
         )
         pl.semaphore_signal(barrier, inc=1, device_id=axis.partner(), device_id_type=MESH)
     load_amps.start()
     load_vir(0, ab).start()
     load_vir(1, cd).start()
     load_occ.start()
-    for q in range(EARLY):
+    for q in range(tiles):
         load(q).start()
     load_amps.wait()
-    mine = fold(amps_held[...].astype(F32))
+    amp_width = size // AMP_CHUNKS
     pl.semaphore_wait(barrier, 2 * GROUP)
-    gather_one.send_group(0, mine)
-    for q in range(EARLY, tiles):
-        load(q).start()
+    for i in range(AMP_CHUNKS):
+        part = amps_held[:, i * amp_width : (i + 1) * amp_width]
+        gather_one.send_group(i, fold(part.astype(F32)))
 
     load_vir(0, ab).wait()
     load_vir(1, cd).wait()
@@ -270,9 +346,27 @@
             )
     acc_two[...] = jnp.zeros_like(acc_two)
     acc_three[...] = jnp.zeros_like(acc_three)
-    gather_one.send_pair(0)
-    gather_one.wait(0)
-    gather_one.write_rows(0, first, 0)
+    def turn(r):
+        load(r).wait()
+
+        def part(c, carry):
+            to, at = (pl.ds(pl.multiple_of(i * TILE, TILE), TILE) for i in (r, c))
+            turned[at, to] = block[to, at].T
+            return carry
+
+        lax.fori_loop(0, tiles, part, 0)
+
+    for r in range(tiles):
+        turn(r)
+    for i in range(AMP_CHUNKS):
+        gather_one.send_pair(i)
+    first_tile = jnp.zeros((rows, TILE), F32)
+    for i in range(AMP_CHUNKS):
+        gather_one.wait(i)
+        gather_one.write_rows(i, first, i * amp_width)
+        at = slice(i * amp_width, (i + 1) * amp_width)
+        first_tile += dot(first[:, at], turned[at, :TILE])
+    acc_one[:, :TILE] = first_tile
 
     def columns(q):
         return pl.ds(pl.multiple_of(q * width, width), width)
@@ -284,27 +378,30 @@
         @pl.when(lax.rem(q, per_tile) == 0)
         def _():
             n = lax.div(q, per_tile)
-            load(n).wait()
-            acc_one[:, tile(n)] = lax.dot_general(
-                first[...], block[tile(n), :], (((1,), (1,)), ((), ())), preferred_element_type=F32
-            )
+
+            @pl.when(n > 0)
+            def _():
+                acc_one[:, tile(n)] = dot(first[...], turned[:, tile(n)])
+
             for i in range(per_tile):
-                scatter_one.send_pair(q + i)
+                scatter_one.begin(q + i)
 
     def store(i):
         return pltpu.make_async_copy(out_held.at[i], outs[i], out_sem.at[i])
 
     def finish(scatter, i, den, gather, q):
-        total = scatter.total(q)
-        if gather is not None:
-            gather.send_group(q, total / den[q])
-        out_held[i, :, columns(q)] = unfold(total).astype(BF16)
+        def use(total):
+            if gather is not None:
+                gather.send_group(q, total / den[q])
+            out_held[i, :, columns(q)] = unfold(total).astype(BF16)
+
+        scatter.end(q, use)
 
         @pl.when(q == CHUNKS - 1)
         def _():
             store(i).start()
 
-    def product(gather, scatter, acc, over_rows, q):
+    def product(gather, scatter, acc, integrals, q):
         gather.wait(q)
         for i in range(per_tile):
 
@@ -317,22 +414,12 @@
             m = lax.div(q, per_tile)
 
             def part(n, carry):
-                if over_rows:
-                    acc[:, tile(n)] += jnp.dot(
-                        chunk[...], block[tile(m), tile(n)], preferred_element_type=F32
-                    )
-                else:
-                    acc[:, tile(n)] += lax.dot_general(
-                        chunk[...],
-                        block[tile(n), tile(m)],
-                        (((1,), (1,)), ((), ())),
-                        preferred_element_type=F32,
-                    )
+                acc[:, tile(n)] += dot(chunk[...], integrals[tile(m), tile(n)])
 
                 @pl.when(q == CHUNKS - 1)
                 def _():
                     for i in range(per_tile):
-                        scatter.send_pair(n * per_tile + i)
+                        scatter.begin(n * per_tile + i)
 
                 return carry
 
@@ -343,27 +430,27 @@
         s4 + CHUNKS,
         (
             (s0, product_one),
-            (s1, scatter_one.send_group),
+            (s1, scatter_one.middle),
             (s2, functools.partial(finish, scatter_one, 0, den_second, gather_two)),
             (s3, gather_two.send_pair),
-            (s4, functools.partial(product, gather_two, scatter_two, acc_two, True)),
+            (s4, functools.partial(product, gather_two, scatter_two, acc_two, block)),
         ),
     )
     s0, s1, s2, s3 = STAGES_TWO
     staged(
         s3 + CHUNKS,
         (
-            (s0, scatter_two.send_group),
+            (s0, scatter_two.middle),
             (s1, functools.partial(finish, scatter_two, 1, den_first, gather_three)),
             (s2, gather_three.send_pair),
-            (s3, functools.partial(product, gather_three, scatter_three, acc_three, False)),
+            (s3, functools.partial(product, gather_three, scatter_three, acc_three, turned)),
         ),
     )
     s0, s1 = STAGES_THREE
     staged(
         s1 + CHUNKS,
         (
-            (s0, scatter_three.send_group),
+            (s0, scatter_three.middle),
             (s1, functools.partial(finish, scatter_three, 2, None, None)),
         ),
     )
@@ -391,18 +478,17 @@
     size = integrals.shape[0]
     width = size // CHUNKS
     rows = occ_energy.shape[0]
-    scatter = Scatter.scratch(CHUNKS, width)
-    gather = Gather.scratch(CHUNKS, width)
     hbm = pl.BlockSpec(memory_space=pltpu.HBM)
     out = jax.ShapeDtypeStruct(amplitudes.shape, BF16)
     ladders = pl.pallas_call(
-        functools.partial(kernel, len(scatter), len(gather)),
+        kernel,
         out_shape=(out, out, out),
         in_specs=[hbm] * 4,
         out_specs=(hbm, hbm, hbm),
         scratch_shapes=[
             pltpu.VMEM(amplitudes.shape, BF16),
             pltpu.SMEM((rows,), F32),
+            pltpu.VMEM((size, size), BF16),
             pltpu.VMEM((size, size), BF16),
             pltpu.SemaphoreType.DMA((size // TILE,)),
             pltpu.VMEM((2, size // LANES, LANES), F32),
@@ -415,9 +501,11 @@
             pltpu.SemaphoreType.DMA((3,)),
         ]
         + [pltpu.VMEM((rows, size), F32)] * 3
-        + scatter * 3
-        + Gather.scratch(1, size)
-        + gather * 2,
+        + Scatter.scratch(CHUNKS, width, WIDE_ONE)
+        + Scatter.scratch(CHUNKS, width, ())
+        + Scatter.scratch(CHUNKS, width, WIDE_THREE)
+        + Gather.scratch(AMP_CHUNKS, size // AMP_CHUNKS)
+        + Gather.scratch(CHUNKS, width) * 2,
         compiler_params=pltpu.CompilerParams(
             collective_id=0, has_side_effects=True, vmem_limit_bytes=VMEM_LIMIT
         ),

time: 70 us -> 65.9 us (0.941)
  Pallas kernels: 69.2 us -> 64.8 us
    pallas_call x1, Pallas kernels: 67.7 us -> 63.4 us  [per_device(): pl.pallas_call(kernel, out_shape=(out, out, out), in_specs=[hbm] * 4, out...]
where the time goes in v3:
time: 65.9 us; the launch traced here: 65.5 us
  Pallas kernels  64.8 us (98%)
    pallas_call x1, Pallas kernels, per_device(): pl.pallas_call(kernel, out_shape=(out, out, out), in_specs=[hbm] * 4, out...  63.4 us
    pallas_call x1, Pallas kernels, per_device(): pl.pallas_call(hand_on, out_shape=(out, out, out), in_specs=[hbm] * 3, ou...  1.43 us

profile of v3, /device:TPU:8, one launch (start us, length us, event | category | flops | bytes accessed | tf_op | source)
XLA Modules:
  0.0 65.5 jit_solution(396581750220287199)
XLA Ops:
  0.6 63.4 %ladder.1 = (bf16[8,2048]{1,0:T(8,128)(2,1)}, bf16[8,2048]{1,0:T(8,128)(2,1)}, bf16[8,2048]{1,0:T(8,128)(2,1)}) custom-call(bf16[8,2048]{1,0:T(8,128)(2,1)} %amps.1, bf16[2048,2048]{1,0:T(8,128)(2,1)} %integrals.1, f32[256,128]{1,0:T(8,128)} %bitcast.1, f32[128]{0:T(128)} %occ.1), custom_call_target="tpu_custom_call" | custom-call | flops 3221225472 | bytes 8388608 | tf_op jit(solution)/shard_map/ladder/pallas_call | solution.py:483
  64.0 1.4 %hand_on.1 = (bf16[8,2048]{1,0:T(8,128)(2,1)}, bf16[8,2048]{1,0:T(8,128)(2,1)}, bf16[8,2048]{1,0:T(8,128)(2,1)}) custom-call(bf16[8,2048]{1,0:T(8,128)(2,1)} %get-tuple-element.6.refs_0_, bf16[8,2048]{1,0:T(8,128)(2,1)} %get-tuple-element.7.refs_1_, bf16[8,2048]{1,0:T(8,128)(2,1)} %get-tuple-element.8.refs_2_), custom_call_target="tpu_custom_call" | custom-call | tf_op jit(solution)/shard_map/hand_on/pallas_call | solution.py:517

commit v4 on v3

--- a/solution.py
+++ b/solution.py
@@ -2,6 +2,7 @@
 
 import jax
 import jax.numpy as jnp
+import numpy as np
 from jax import lax
 from jax.experimental import pallas as pl
 from jax.experimental.pallas import tpu as pltpu
@@ -103,7 +104,7 @@
         return out
 
     def columns(self, q):
-        return pl.ds(pl.multiple_of(q * self.width, self.width), self.width)
+        return pl.ds(q * self.width if isinstance(q, int) else pl.multiple_of(q * self.width, self.width), self.width)
 
     def rows(self, q, g, pair):
         at = pl.ds(pl.multiple_of(g * 16 + pair * ROWS, ROWS), ROWS)
@@ -112,10 +113,10 @@
     def either(self, q, narrow, wide):
         is_wide = False
         for i, w in enumerate(self.wide):
-            pl.when(q == w)(functools.partial(wide, i))
+            when(q == w)(functools.partial(wide, i))
             is_wide = (q == w) | is_wide
         if self.wide:
-            pl.when(jnp.logical_not(is_wide))(narrow)
+            when(not is_wide if isinstance(is_wide, bool) else jnp.logical_not(is_wide))(narrow)
         else:
             narrow()
 
@@ -262,17 +263,17 @@
         wait_bytes(self.held.at[:, 0, pl.ds(0, GROUP - 1)], self.sent.at[1])
 
 
+def when(cond):
+    if isinstance(cond, (bool, np.bool_)):
+        return (lambda f: f()) if cond else (lambda f: None)
+    return pl.when(cond)
+
+
 def staged(steps, stages):
-    def body(t, carry):
+    for t in range(steps):
         for start, run in stages:
-
-            @pl.when((t >= start) & (t < start + CHUNKS))
-            def _():
+            if start <= t < start + CHUNKS:
                 run(t - start)
-
-        return carry
-
-    lax.fori_loop(0, steps, body, 0)
 
 
 def kernel(amps, integrals, vir, occ, one, two, three, *scratch):
@@ -369,17 +370,17 @@
     acc_one[:, :TILE] = first_tile
 
     def columns(q):
-        return pl.ds(pl.multiple_of(q * width, width), width)
+        return pl.ds(q * width if isinstance(q, int) else pl.multiple_of(q * width, width), width)
 
     def tile(n):
-        return pl.ds(pl.multiple_of(n * TILE, TILE), TILE)
+        return pl.ds(n * TILE if isinstance(n, int) else pl.multiple_of(n * TILE, TILE), TILE)
 
     def product_one(q):
-        @pl.when(lax.rem(q, per_tile) == 0)
+        @when((q % per_tile) == 0)
         def _():
-            n = lax.div(q, per_tile)
-
-            @pl.when(n > 0)
+            n = (q // per_tile)
+
+            @when(n > 0)
             def _():
                 acc_one[:, tile(n)] = dot(first[...], turned[:, tile(n)])
 
@@ -397,7 +398,7 @@
 
         scatter.end(q, use)
 
-        @pl.when(q == CHUNKS - 1)
+        @when(q == CHUNKS - 1)
         def _():
             store(i).start()
 
@@ -405,25 +406,24 @@
         gather.wait(q)
         for i in range(per_tile):
 
-            @pl.when(lax.rem(q, per_tile) == i)
+            @when((q % per_tile) == i)
             def _():
                 gather.write_rows(q, chunk, i * width)
 
-        @pl.when(lax.rem(q, per_tile) == per_tile - 1)
+        @when((q % per_tile) == per_tile - 1)
         def _():
-            m = lax.div(q, per_tile)
-
-            def part(n, carry):
+            m = (q // per_tile)
+
+            def part(n):
                 acc[:, tile(n)] += dot(chunk[...], integrals[tile(m), tile(n)])
 
-                @pl.when(q == CHUNKS - 1)
+                @when(q == CHUNKS - 1)
                 def _():
                     for i in range(per_tile):
                         scatter.begin(n * per_tile + i)
 
-                return carry
-
-            lax.fori_loop(0, tiles, part, 0)
+            for n in range(tiles):
+                part(n)
 
     s0, s1, s2, s3, s4 = STAGES_ONE
     staged(

time: 65.9 us -> 65.5 us (level)
  Pallas kernels: 64.8 us -> 64 us
    pallas_call x1, Pallas kernels: 63.4 us -> 62.5 us  [per_device(): pl.pallas_call(kernel, out_shape=(out, out, out), in_specs=[hbm] * 4, out...]
where the time goes in v4:
time: 65.5 us; the launch traced here: 64.6 us
  Pallas kernels  64 us (98%)
    pallas_call x1, Pallas kernels, per_device(): pl.pallas_call(kernel, out_shape=(out, out, out), in_specs=[hbm] * 4, out...  62.5 us
    pallas_call x1, Pallas kernels, per_device(): pl.pallas_call(hand_on, out_shape=(out, out, out), in_specs=[hbm] * 3, ou...  1.43 us

profile of v4, /device:TPU:8, one launch (start us, length us, event | category | flops | bytes accessed | tf_op | source)
XLA Modules:
  0.0 64.6 jit_solution(796644391518704877)
XLA Ops:
  0.6 62.5 %ladder.1 = (bf16[8,2048]{1,0:T(8,128)(2,1)}, bf16[8,2048]{1,0:T(8,128)(2,1)}, bf16[8,2048]{1,0:T(8,128)(2,1)}) custom-call(bf16[8,2048]{1,0:T(8,128)(2,1)} %amps.1, bf16[2048,2048]{1,0:T(8,128)(2,1)} %integrals.1, f32[256,128]{1,0:T(8,128)} %bitcast.1, f32[128]{0:T(128)} %occ.1), custom_call_target="tpu_custom_call" | custom-call | flops 3221225472 | bytes 8388608 | tf_op jit(solution)/shard_map/ladder/pallas_call | solution.py:483
  63.2 1.4 %hand_on.1 = (bf16[8,2048]{1,0:T(8,128)(2,1)}, bf16[8,2048]{1,0:T(8,128)(2,1)}, bf16[8,2048]{1,0:T(8,128)(2,1)}) custom-call(bf16[8,2048]{1,0:T(8,128)(2,1)} %get-tuple-element.6.refs_0_, bf16[8,2048]{1,0:T(8,128)(2,1)} %get-tuple-element.7.refs_1_, bf16[8,2048]{1,0:T(8,128)(2,1)} %get-tuple-element.8.refs_2_), custom_call_target="tpu_custom_call" | custom-call | tf_op jit(solution)/shard_map/hand_on/pallas_call | solution.py:517

commit v5 on v4

--- a/solution.py
+++ b/solution.py
@@ -345,8 +345,6 @@
             den[q, side * ROWS : (side + 1) * ROWS, at * LANES : (at + 1) * LANES] = (
                 jnp.broadcast_to(vir_held[i, lane_tile : lane_tile + 1, :], (ROWS, LANES)) - levels
             )
-    acc_two[...] = jnp.zeros_like(acc_two)
-    acc_three[...] = jnp.zeros_like(acc_three)
     def turn(r):
         load(r).wait()
 
@@ -415,7 +413,8 @@
             m = (q // per_tile)
 
             def part(n):
-                acc[:, tile(n)] += dot(chunk[...], integrals[tile(m), tile(n)])
+                term = dot(chunk[...], integrals[tile(m), tile(n)])
+                acc[:, tile(n)] = term if m == 0 else acc[:, tile(n)] + term
 
                 @when(q == CHUNKS - 1)
                 def _():

time: 65.5 us -> 65.7 us (level)
  no operation moved by 1% of the time
where the time goes in v5:
time: 65.7 us; the launch traced here: 64.6 us
  Pallas kernels  64 us (97%)
    pallas_call x1, Pallas kernels, per_device(): pl.pallas_call(kernel, out_shape=(out, out, out), in_specs=[hbm] * 4, out...  62.5 us
    pallas_call x1, Pallas kernels, per_device(): pl.pallas_call(hand_on, out_shape=(out, out, out), in_specs=[hbm] * 3, ou...  1.43 us

profile of v5, /device:TPU:8, one launch (start us, length us, event | category | flops | bytes accessed | tf_op | source)
XLA Modules:
  0.0 64.6 jit_solution(2325853772549936582)
XLA Ops:
  0.6 62.5 %ladder.1 = (bf16[8,2048]{1,0:T(8,128)(2,1)}, bf16[8,2048]{1,0:T(8,128)(2,1)}, bf16[8,2048]{1,0:T(8,128)(2,1)}) custom-call(bf16[8,2048]{1,0:T(8,128)(2,1)} %amps.1, bf16[2048,2048]{1,0:T(8,128)(2,1)} %integrals.1, f32[256,128]{1,0:T(8,128)} %bitcast.1, f32[128]{0:T(128)} %occ.1), custom_call_target="tpu_custom_call" | custom-call | flops 3221225472 | bytes 8388608 | tf_op jit(solution)/shard_map/ladder/pallas_call | solution.py:482
  63.2 1.4 %hand_on.1 = (bf16[8,2048]{1,0:T(8,128)(2,1)}, bf16[8,2048]{1,0:T(8,128)(2,1)}, bf16[8,2048]{1,0:T(8,128)(2,1)}) custom-call(bf16[8,2048]{1,0:T(8,128)(2,1)} %get-tuple-element.6.refs_0_, bf16[8,2048]{1,0:T(8,128)(2,1)} %get-tuple-element.7.refs_1_, bf16[8,2048]{1,0:T(8,128)(2,1)} %get-tuple-element.8.refs_2_), custom_call_target="tpu_custom_call" | custom-call | tf_op jit(solution)/shard_map/hand_on/pallas_call | solution.py:516
